TPU v7x, 512 devices: a whole 4x4x16 slice. The times are simulated.
512 devices in a mesh: mem: 64 (over x_hi, z, core), hist: 8 (over y, x_lo).
Axes of the slice: x: 4 (x_hi: 2, x_lo: 2; x = x_hi * 2 + x_lo), y: 4, z: 16, core: 2. Of those that a mesh axis runs over, the one named last changes fastest.
Arguments:
- memory_block: bfloat16 [256, 64, 64, 128], P('mem', 'hist'), may hold values from -1.5 to 1.5
- memory_rows: bfloat16 [131072, 2, 128], P(('mem', 'hist')), may hold values from -6 to 6
- panel_rows: bfloat16 [32768, 2, 128], P(('hist', 'mem')), may hold values from -6 to 6
- time_deal: int32 [256], replicated, may hold values from 0 to 255, each once
- column_times: int32 [64], replicated, may hold values from 0 to 255
- window_start: int32 [1], replicated, may hold values from 0 to 128
- coupling: float32 [64, 64], replicated, may hold values from -0.375 to 0.375
- hamiltonian: bfloat16 [64, 64], replicated, may hold values from -6 to 6
Outputs:
- new_rows: bfloat16 [32768, 2, 128], P(('hist', 'mem'))
- new_sigma: bfloat16 [32768, 2, 128], P(('hist', 'mem'))
Inputs may be any that keep to these rules, and one draw needn't show every extreme that they name: `time_deal`: each of 0 to 255 once.
All inputs are finite; a program needn't handle non-finite values.
Results may differ from a plain program's by a relative error of at most 0.014.
Values may be sent and summed in bfloat16 or wider, within the bound.
A program may use at most 64 MiB of HBM per device.

v0:
```python
import jax
import jax.numpy as jnp
from jax import lax
from jax.sharding import PartitionSpec as P

P_SIZE = 8


time_step = 0.02


def sigma_of(tiles, coupling):
    orbitals = coupling.shape[0]
    real_part = tiles[..., :orbitals]
    imag_part = tiles[..., orbitals:]
    bubble = real_part * real_part + imag_part * imag_part
    screened = jnp.einsum("ik,...kpl->...ipl", coupling, bubble, precision=lax.Precision.HIGHEST)
    screening = jnp.einsum("...ipl,jl->...ipj", screened, coupling, precision=lax.Precision.HIGHEST)
    return -jnp.concatenate([real_part * screening, imag_part * screening], -1)


def row_sigma(row_block, coupling):
    orbitals = coupling.shape[0]
    shaped = row_block.astype(jnp.float32).reshape(
        -1, orbitals, row_block.shape[1], row_block.shape[2]
    )
    result = sigma_of(shaped, coupling).astype(jnp.bfloat16)
    return result.reshape(row_block.shape)


def complex_form(tiles):
    orbitals = tiles.shape[-1] // 2
    real_part = tiles[..., :orbitals]
    imag_part = tiles[..., orbitals:]
    upper = jnp.concatenate([real_part, imag_part], -1)
    lower = jnp.concatenate([-imag_part, real_part], -1)
    return jnp.concatenate([upper, lower], -2)


def advance(row_block, collision, hamiltonian):
    orbitals = hamiltonian.shape[0]
    shaped = row_block.reshape(-1, orbitals, row_block.shape[1], row_block.shape[2])
    applied = jnp.einsum("ik,nkpc->nipc", hamiltonian, shaped, preferred_element_type=jnp.float32)
    turned = jnp.concatenate([applied[..., orbitals:], -applied[..., :orbitals]], -1)
    summed = turned.reshape(row_block.shape) + collision
    return (row_block.astype(jnp.float32) + time_step * summed).astype(jnp.bfloat16)


def local(
    memory_block,
    memory_rows,
    panel_rows,
    time_deal,
    column_times,
    window_start,
    coupling,
    hamiltonian,
):
    orbitals = coupling.shape[0]
    panels = panel_rows.shape[1]
    slots = memory_block.shape[0]
    columns = memory_block.shape[1]
    mem_index = lax.axis_index("mem")
    hist_index = lax.axis_index("hist")
    tile_rows = P_SIZE * orbitals
    own_rows = panel_rows.shape[0]
    gathered = lax.all_gather(memory_rows, "hist", axis=0, tiled=True)
    slot_sigma = row_sigma(gathered, coupling)
    slot_sigma = slot_sigma.reshape(slots, P_SIZE, orbitals, panels, 2 * orbitals)
    slot_times = lax.dynamic_slice_in_dim(time_deal, mem_index * slots, slots, 0)
    local_columns = lax.dynamic_slice_in_dim(column_times, hist_index * columns, columns, 0)
    causal = (slot_times[:, None] >= local_columns[None, :]) & (
        slot_times[:, None] >= window_start[0]
    )
    forms = complex_form(memory_block) * causal[:, :, None, None].astype(jnp.bfloat16)
    count = columns * tile_rows
    tiles = count // orbitals
    tile_ids = 0 // orbitals + jnp.arange(tiles, dtype=jnp.int32)
    picked_sigma = jnp.take(slot_sigma, tile_ids % P_SIZE, axis=1)
    picked_forms = jnp.take(forms, tile_ids // P_SIZE, axis=1)
    term = jnp.einsum(
        "kqipr,kqrc->qipc", picked_sigma, picked_forms, preferred_element_type=jnp.float32
    )
    summed = lax.psum(term.reshape(count, panels, 2 * orbitals), "mem")
    own_sum = lax.dynamic_slice_in_dim(summed, mem_index * own_rows, own_rows, 0)
    advanced = advance(panel_rows, own_sum, hamiltonian)
    new_sigma = row_sigma(advanced, coupling)
    return (advanced, new_sigma)


def solution(mesh):
    in_specs = (
        P("mem", "hist", None, None),
        P(("mem", "hist"), None, None),
        P(("hist", "mem"), None, None),
        P(),
        P(),
        P(),
        P(),
        P(),
    )
    out_specs = (P(("hist", "mem"), None, None), P(("hist", "mem"), None, None))
    return jax.shard_map(local, mesh=mesh, in_specs=in_specs, out_specs=out_specs, check_vma=False)
```

profile of v0, /device:TPU:6, one launch (start us, length us, event | category | flops | bytes accessed | tf_op | source)
XLA Modules:
  0.0 626.4 jit_solution(14973034443334457640)
XLA Ops:
  7.2 0.0 copy-start
  7.2 0.0 copy-start.1
  7.2 0.0 all-gather.2.cloned.1.call-start
  7.2 1.6 copy.19
  8.9 0.0 all-gather.2.cloned.1.call-update
  8.9 0.0 all-reduce.2.cloned.1.call-start
  9.6 0.7 dynamic_slice.10
  10.3 0.8 broadcast_compare_fusion
  11.1 0.1 and_convert_fusion
  11.2 1.4 slice_negate_fusion
  12.6 0.0 copy-done.1
  12.6 0.5 maximum_multiply_fusion
  13.1 5.5 gather_fusion.1
  18.7 41.9 %all-gather.2.cloned.1.call-done = bf16[2048,2,128]{2,0,1:T(8,128)(2,1)} async-done(((bf16[256,2,128]{2,0,1:T(8,128)(2,1)}), bf16[2048,2,128]{2,0,1:T(8,128)(2,1)}) %all-gather.2.cloned.1.call-update) | async-done | bytes 1048592 | tf_op jit(solution)/shard_map/all_gather | solution.py:67
  60.5 2.3 fusion.36
  62.8 0.0 copy-done
  62.8 2.3 fusion.9
  65.1 1.9 copy_multiply_fusion.1
  67.0 0.6 fusion.6
  67.6 5.2 gather_fusion
  72.9 10.2 %fusion = f32[64,64,2,128,1]{3,1,4,0,2:T(8,128)} fusion(bf16[64,4,128,128]{3,2,1,0:T(8,128)(2,1)} %gather_fusion.1, pred[64]{0:T(512)(128)(4,1)S(1)} %compare_and_fusion, bf16[64,4,64,2,128]{4,2,3,1,0:T(8,128)(2,1)} %gather_fusion, pred[64]{0:T(512)(128)(4,1)S(1)} %compare_and_fusion.1), kind=kOutput, calls=%fused_computation.2 | convolution fusion | flops 1082130432 | bytes 20971648 | tf_op jit(solution)/shard_map/kqipr,kqrc->qipc/dot_general | solution.py:81
  83.0 0.0 copy-start.2
  83.0 0.0 copy-start.3
  83.0 0.0 all-reduce.2.cloned.1.call-update
  83.1 0.7 copy-done.2
  83.8 0.0 copy-done.3
  83.8 0.1 convolution_bitcast_fusion
  83.9 0.1 fusion.37
  84.0 532.6 %all-reduce.2.cloned.1.call-done = f32[4096,2,128]{2,0,1:T(8,128)} async-done(((f32[4096,2,128]{2,0,1:T(8,128)}), f32[4096,2,128]{2,0,1:T(8,128)}) %all-reduce.2.cloned.1.call-update) | async-done | bytes 4194320 | tf_op jit(solution)/shard_map/psum | solution.py:84
  616.6 0.9 bitcast_convert_fusion
  617.5 0.4 convolution_bitcast_fusion.2
  617.9 0.3 multiply_bitcast_fusion.1
  618.2 0.1 fusion.19
  618.3 0.7 copy.27
  618.9 0.6 copy.26
  (6 shorter events, 0.0 us)
Async XLA Ops:
  7.2 55.7 %copy-start = (f32[64,64]{1,0:T(8,128)S(1)}, f32[64,64]{1,0:T(8,128)}, u32[]{:S(2)}) copy-start(f32[64,64]{1,0:T(8,128)} %param.14) | copy-start | bytes 49156
  7.2 5.4 copy-start.1
  7.2 53.3 %all-gather.2.cloned.1.call-start = ((), (), s32[]{:S(2)}) async-start(), calls=%async_computation | async-start | bytes 1179648 | tf_op jit(solution)/shard_map/all_gather | solution.py:67
  8.9 607.7 %all-reduce.2.cloned.1.call-start = ((), (), s32[]{:S(2)}) async-start(), calls=%async_computation.1 | async-start | bytes 8388608 | tf_op jit(solution)/shard_map/psum | solution.py:84
  83.0 0.8 copy-start.2
  83.0 0.8 copy-start.3
Sparse Core Ops, SparseCore 0:
  10.1 50.3 all-gather.1
  83.2 533.3 all-reduce.1
where the time goes:
time: 629 us; the launch traced here: 626 us
  waiting for transfers between devices  574 us (91%)
  local copies, waits for them, and re-layouts  17.5 us (3%)
  matrix products  15.1 us (2%)
  between operations  14.8 us (2%)
    psum x1, waiting for transfers between devices, local(): summed = lax.psum(term.reshape(count, panels, 2 * orbitals), 'mem')  533 us
    all_gather x1, waiting for transfers between devices, local(): gathered = lax.all_gather(memory_rows, 'hist', axis=0, tiled=True)  41.9 us
  transfers between devices with their start and end apart: 2, of which 2 were waited for; matrix products, arithmetic and copies ran while one was open for 1% of the time, Pallas kernels for 0%

commit v1 on v0

v1 whole, which is shorter than its diff:
```python
import jax
import jax.numpy as jnp
from jax import lax
from jax.experimental import pallas as pl
from jax.experimental.pallas import tpu as pltpu
from jax.sharding import PartitionSpec as P


MESH = pl.DeviceIdType.MESH
BF16 = jnp.bfloat16
F32 = jnp.float32
P_SIZE = 8
TIME_STEP = 0.02
NZ = 16
NY = 4
HALF = NZ // 2


def halves(x):
    high = x.astype(BF16)
    return high, (x - high.astype(F32)).astype(BF16)


def dot(a, b):
    return jnp.dot(a, b, preferred_element_type=F32)


def chosen(shape, test):
    rows = lax.broadcasted_iota(jnp.int32, shape, 0)
    columns = lax.broadcasted_iota(jnp.int32, shape, 1)
    return jnp.where(test(rows, columns), 1.0, 0.0).astype(BF16)


def pair_form(small):
    spread = chosen((128, 64), lambda r, c: (r >> 1) == c)
    gather = chosen((64, 128), lambda r, c: r == (c >> 1))
    wide = dot(dot(spread, small).astype(BF16), gather)
    same = chosen((128, 128), lambda r, c: (r & 1) == (c & 1))
    return wide.astype(BF16) * same


def lane_form(small):
    spread = chosen((128, 64), lambda r, c: (r & 63) == c)
    gather = chosen((64, 128), lambda r, c: r == (c & 63))
    turned = lax.dot_general(spread, small, (((1,), (1,)), ((), ())), preferred_element_type=F32)
    return dot(turned.astype(BF16), gather).astype(BF16)


def sigma_of(x, left, right):
    count = x.shape[0] // 128
    wide = x.astype(F32)
    high, low = halves(wide * wide)
    over = dot(jnp.concatenate([high, low, high], axis=1), right)
    high, low = halves(over)
    result = []
    for n in range(count):
        rows = slice(n * 128, (n + 1) * 128)
        stacked = jnp.concatenate([high[rows], low[rows], high[rows]], axis=0)
        result.append(-(wide[rows] * dot(left, stacked)))
    return result


def kernel(
    time_deal, column_times, window_start, block_ref, memory_ref, panel_ref, coupling_ref, hamiltonian_ref,
    rows_ref, sigma_ref,
    blocks, forms, own_sigma, old_sigma, partial, up_in, up_out, down_in, down_out, last_in, cross_out,
    block_sem, core_sem, y_sem, x_sem, y2_sem, xy_sem, x2_sem,
    up_sem, down_sem, last_sem, cross_sem,
    block_send, core_send, y_send, x_send, y2_send, xy_send, x2_send, up_send, down_send,
):
    mem = lax.axis_index("mem")
    hist = lax.axis_index("hist")
    core = lax.rem(mem, 2)
    z = lax.rem(lax.div(mem, 2), NZ)
    x_hi = lax.div(mem, 2 * NZ)
    y = lax.div(hist, 2)
    x_lo = lax.rem(hist, 2)
    chip = mem - core
    y_next = (lax.rem(y + 1, NY), lax.rem(y + NY - 1, NY))
    y_far = lax.rem(y + 2, NY)
    z_next = (lax.rem(z + 1, NZ), lax.rem(z + NZ - 1, NZ))

    def at_mem(xx, zz):
        return xx * (2 * NZ) + zz * 2 + core

    def at_hist(yy, xx):
        return yy * 2 + xx

    def send(src, dst, send_sem, recv_sem, where):
        copy = pltpu.make_async_remote_copy(
            src_ref=src, dst_ref=dst, send_sem=send_sem, recv_sem=recv_sem, device_id=where, device_id_type=MESH
        )
        return copy

    other_x = at_hist(y, 1 - x_lo)
    peers = [(chip + 1 - core, hist)]
    peers += [(chip + q, other_x) for q in range(2)]
    peers += [(chip + q, at_hist(yy, x_lo)) for yy in y_next for q in range(2)]
    peers += [(at_mem(xx, zz), hist) for xx in range(2) for zz in z_next]
    peers += [(at_mem(1 - x_hi, z), hist)]
    barrier = pltpu.get_barrier_semaphore()
    for peer in peers:
        pl.semaphore_signal(barrier, inc=1, device_id=peer, device_id_type=MESH)

    block_here = pltpu.make_async_copy(block_ref, blocks.at[core], block_send.at[0])
    block_here.start()

    coupling_high, coupling_low = halves(coupling_ref[...])
    left_high, left_low = pair_form(coupling_high), pair_form(coupling_low)
    left = jnp.concatenate([left_high, left_high, left_low], axis=1)
    right_high, right_low = lane_form(coupling_high), lane_form(coupling_low)
    right = jnp.concatenate([right_high, right_high, right_low], axis=0)
    for u, tile in enumerate(sigma_of(memory_ref[...], left, right)):
        own_sigma[u % 2, u // 2] = tile.astype(BF16)

    pl.semaphore_wait(barrier, len(peers))

    mine = core * NY + y
    first = []
    first.append(send(own_sigma.at[1 - core], old_sigma.at[x_lo, mine], core_send, core_sem, (chip + 1 - core, hist)))
    for q in range(2):
        for d in range(2):
            first.append(
                send(own_sigma.at[q], old_sigma.at[x_lo, mine], y_send.at[d, q], y_sem.at[d, core],
                     (chip + q, at_hist(y_next[d], x_lo)))
            )
        first.append(send(own_sigma.at[q], old_sigma.at[x_lo, mine], x_send.at[q], x_sem.at[core], (chip + q, other_x)))
    block_there = send(block_ref, blocks.at[core], block_send.at[1], block_sem, (chip + 1 - core, hist))
    for copy in first:
        copy.start()
    block_there.start()
    old_sigma[x_lo, mine] = own_sigma[core]

    def arrived(dst, sem):
        send(dst, dst, sem, sem, peers[0]).wait_recv()

    sign = jnp.where(lax.broadcasted_iota(jnp.int32, (64, 128), 1) < 64, -1.0, 1.0)
    start = window_start[0]

    def build(which):
        for k in range(4):
            slot_time = time_deal[(chip + which) * 4 + k]
            for j in range(8):
                keep = (slot_time >= column_times[hist * 8 + j]) & (slot_time >= start)
                level = jnp.where(keep, 1.0, 0.0)
                tile = blocks[which, k, j].astype(F32) * level
                row = pl.multiple_of((which * 4 + k) * 128, 128)
                forms[pl.ds(row, 64), j * 128 : (j + 1) * 128] = tile.astype(BF16)
                forms[pl.ds(row + 64, 64), j * 128 : (j + 1) * 128] = (pltpu.roll(tile, 64, 1) * sign).astype(BF16)

    block_here.wait()
    build(core)

    panel = panel_ref[...]
    applied = dot(pair_form(hamiltonian_ref[...]), panel)
    turned = pltpu.roll(applied, 64, 1) * jnp.where(lax.broadcasted_iota(jnp.int32, (128, 128), 1) < 64, 1.0, -1.0)
    base = panel.astype(F32) + TIME_STEP * turned

    block_there.wait_recv()
    build(1 - core)

    second = []
    for q in range(2):
        for d in range(2):
            kk = q * NY + y_next[1 - d]
            arrived(old_sigma.at[x_lo, kk], y_sem.at[d, q])
            copy = send(old_sigma.at[x_lo, kk, d], old_sigma.at[x_lo, kk, d], y2_send.at[d, q], y2_sem.at[d, q],
                        (mem, at_hist(y_next[d], x_lo)))
            copy.start()
            second.append(copy)
    for q in range(2):
        kk = q * NY + y
        arrived(old_sigma.at[1 - x_lo, kk], x_sem.at[q])
        for d in range(2):
            copy = send(old_sigma.at[1 - x_lo, kk], old_sigma.at[1 - x_lo, kk], xy_send.at[d, q], xy_sem.at[d, q],
                        (mem, at_hist(y_next[d], x_lo)))
            copy.start()
            second.append(copy)
    for q in range(2):
        for d in range(2):
            kk = q * NY + y_far
            arrived(old_sigma.at[x_lo, kk, d], y2_sem.at[d, q])
            copy = send(old_sigma.at[x_lo, kk, d], old_sigma.at[x_lo, kk, d], x2_send.at[d, q], x2_sem.at[d, q],
                        (mem, other_x))
            copy.start()
            second.append(copy)
    arrived(old_sigma.at[x_lo, (1 - core) * NY + y], core_sem)

    def multiply(xx):
        lhs = jnp.concatenate(
            [jnp.concatenate([old_sigma[xx, kk, u] for kk in range(8)], axis=1) for u in range(2)], axis=0
        )
        for j in range(4):
            columns = slice(j * 256, (j + 1) * 256)
            product = dot(lhs, forms[:, columns])
            for u in range(2):
                for i in range(2):
                    partial[xx * 2 + u, 2 * j + i] = product[u * 128 : (u + 1) * 128, i * 128 : (i + 1) * 128]

    multiply(x_lo)
    for q in range(2):
        for d in range(2):
            arrived(old_sigma.at[1 - x_lo, q * NY + y_next[1 - d]], xy_sem.at[d, q])
    for q in range(2):
        for d in range(2):
            arrived(old_sigma.at[1 - x_lo, q * NY + y_far, d], x2_sem.at[d, q])
    multiply(1 - x_lo)

    def term(zz, xx):
        return partial[lax.rem(zz, 4), 4 * xx + lax.div(zz, 4)]

    third = []
    cross_out[...] = term(z, 1 - x_hi).astype(BF16)
    copy = send(cross_out, last_in.at[4], cross_sem, last_sem.at[4], (at_mem(1 - x_hi, z), hist))
    copy.start()
    third.append(copy)
    for s in range(HALF):
        for b in range(2):
            for d, steps, came, went, in_sem, out_sem in (
                (0, HALF, up_in, up_out, up_sem, up_send),
                (1, HALF - 1, down_in, down_out, down_sem, down_send),
            ):
                if s >= steps:
                    continue
                far = lax.rem(z + HALF - s, NZ) if d == 0 else lax.rem(z + NZ - (HALF - 1) + s, NZ)
                value = term(far, b)
                if s > 0:
                    arrived(came.at[s - 1, b], in_sem.at[s - 1, b])
                    value = value + came[s - 1, b].astype(F32)
                went[s, b] = value.astype(BF16)
                if s < steps - 1:
                    copy = send(went.at[s, b], came.at[s, b], out_sem.at[s, b], in_sem.at[s, b],
                                (at_mem(x_hi, z_next[d]), hist))
                else:
                    copy = send(went.at[s, b], last_in.at[d * 2 + x_hi], out_sem.at[s, b], last_sem.at[d * 2 + x_hi],
                                (at_mem(b, z_next[d]), hist))
                copy.start()
                third.append(copy)

    total = term(z, x_hi)
    for n in (4, 2, 3, 0, 1):
        arrived(last_in.at[n], last_sem.at[n])
        total = total + last_in[n].astype(F32)
    advanced = (base + TIME_STEP * total).astype(BF16)
    rows_ref[...] = advanced
    [new_sigma] = sigma_of(advanced, left, right)
    sigma_ref[...] = new_sigma.astype(BF16)

    for copy in first + [block_there] + second + third:
        copy.wait_send()


def local(memory_block, memory_rows, panel_rows, time_deal, column_times, window_start, coupling, hamiltonian):
    tile = (128, 128)
    dma = pltpu.SemaphoreType.DMA
    vmem = pl.BlockSpec(memory_space=pltpu.VMEM)
    smem = pl.BlockSpec(memory_space=pltpu.SMEM)
    new_rows, new_sigma = pl.pallas_call(
        kernel,
        out_shape=[jax.ShapeDtypeStruct(tile, BF16)] * 2,
        in_specs=[smem, smem, smem, pl.BlockSpec(memory_space=pl.ANY), vmem, vmem, vmem, vmem],
        out_specs=[vmem, vmem],
        scratch_shapes=[
            pltpu.VMEM((2, 4, 8, 64, 128), BF16),
            pltpu.VMEM((1024, 1024), BF16),
            pltpu.VMEM((2, 2, *tile), BF16),
            pltpu.VMEM((2, 8, 2, *tile), BF16),
            pltpu.VMEM((4, 8, *tile), F32),
            pltpu.VMEM((HALF - 1, 2, *tile), BF16),
            pltpu.VMEM((HALF, 2, *tile), BF16),
            pltpu.VMEM((HALF - 2, 2, *tile), BF16),
            pltpu.VMEM((HALF - 1, 2, *tile), BF16),
            pltpu.VMEM((5, *tile), BF16),
            pltpu.VMEM(tile, BF16),
            dma, dma, dma((2, 2)), dma((2,)), dma((2, 2)), dma((2, 2)), dma((2, 2)),
            dma((HALF - 1, 2)), dma((HALF - 2, 2)), dma((5,)), dma,
            dma((2,)), dma, dma((2, 2)), dma((2,)), dma((2, 2)), dma((2, 2)), dma((2, 2)),
            dma((HALF, 2)), dma((HALF - 1, 2)),
        ],
        compiler_params=pltpu.CompilerParams(
            collective_id=0, has_side_effects=True, vmem_limit_bytes=32 * 2**20
        ),
        cost_estimate=pl.CostEstimate(flops=1100000000, bytes_accessed=2000000, transcendentals=0),
    )(
        time_deal, column_times, window_start, memory_block,
        memory_rows.reshape(512, 128), panel_rows.reshape(128, 128), coupling, hamiltonian,
    )
    return new_rows.reshape(panel_rows.shape), new_sigma.reshape(panel_rows.shape)


def solution(mesh):
    in_specs = (
        P("mem", "hist", None, None),
        P(("mem", "hist"), None, None),
        P(("hist", "mem"), None, None),
        P(),
        P(),
        P(),
        P(),
        P(),
    )
    out_specs = (P(("hist", "mem"), None, None), P(("hist", "mem"), None, None))
    return jax.shard_map(local, mesh=mesh, in_specs=in_specs, out_specs=out_specs, check_vma=False)
```

time: 629 us -> 63.1 us (0.10)
  waiting for transfers between devices: 574 us -> 0 us
  Pallas kernels: 0 us -> 55.3 us
  matrix products: 15.1 us -> 0 us
  between operations: 14.8 us -> 1.31 us
  local copies, waits for them, and re-layouts: 17.5 us -> 6.07 us
    psum x1 -> x0, waiting for transfers between devices: 533 us -> none  [local(): summed = lax.psum(term.reshape(count, panels, 2 * orbitals), 'mem')]
    pallas_call x0 -> x1, Pallas kernels: none -> 55.3 us  [local(): pl.pallas_call(kernel, out_shape=[jax.ShapeDtypeStruct(tile, BF16)] * 2,...]
    all_gather x1 -> x0, waiting for transfers between devices: 41.9 us -> none  [local(): gathered = lax.all_gather(memory_rows, 'hist', axis=0, tiled=True)]
    dot_general x6 -> x0, matrix products: 15.1 us -> none  [the longest x1 10.2 us: local(): jnp.einsum('kqipr,kqrc->qipc', picked_sigma, picked_forms, preferred_elem...]
    gather x2 -> x0, local copies, waits for them, and re-layouts: 10.8 us -> none  [the longest x1 5.54 us: local(): picked_forms = jnp.take(forms, tile_ids // P_SIZE, axis=1)]
  transfers between devices with their start and end apart: 2 -> 0, of which waited for: 2 -> 0; matrix products, arithmetic and copies ran while one was open for 1% -> 0% of each run, Pallas kernels for 0% -> 0%
where the time goes in v1:
time: 63.1 us; the launch traced here: 62.7 us
  Pallas kernels  55.3 us (88%)
  local copies, waits for them, and re-layouts  6.07 us (10%)
  between operations  1.31 us (2%)
    pallas_call x1, Pallas kernels, local(): pl.pallas_call(kernel, out_shape=[jax.ShapeDtypeStruct(tile, BF16)] * 2,...  55.3 us
    unnamed x16, local copies, waits for them, and re-layouts  6.07 us

profile of v1, /device:TPU:6, one launch (start us, length us, event | category | flops | bytes accessed | tf_op | source)
XLA Modules:
  0.0 62.7 jit_solution(7214824173575826421)
XLA Ops:
  1.3 0.0 copy-start.5
  1.3 0.0 copy-start.6
  1.3 0.7 %copy-done.5 = s32[256]{0:T(256)S(1)} copy-done((s32[256]{0:T(256)S(1)}, s32[256]{0:T(256)}, u32[]{:S(2)}) %copy-start.5) | copy-done | bytes 1048
  2.0 0.0 copy-done.6
  2.0 0.0 copy-start
  2.0 1.0 %copy-done = bf16[4,8,64,128]{3,2,1,0:T(8,128)(2,1)S(1)} copy-done((bf16[4,8,64,128]{3,2,1,0:T(8,128)(2,1)S(1)}, bf16[4,8,64,128]{3,2,1,0:T(8,128)(2,1)}, u32[]{:S(2)}) %copy-start) | copy-done | bytes 524312
  3.0 0.0 copy-start.1
  3.0 0.9 %copy-done.1 = bf16[256,2,128]{2,1,0:T(2,128)(2,1)S(1)} copy-done((bf16[256,2,128]{2,1,0:T(2,128)(2,1)S(1)}, bf16[256,2,128]{2,1,0:T(2,128)(2,1)}, u32[]{:S(2)}) %copy-start.1) | copy-done | bytes 131096
  3.9 0.0 copy-start.2
  3.9 0.8 %copy-done.2 = bf16[64,2,128]{2,1,0:T(2,128)(2,1)S(1)} copy-done((bf16[64,2,128]{2,1,0:T(2,128)(2,1)S(1)}, bf16[64,2,128]{2,1,0:T(2,128)(2,1)}, u32[]{:S(2)}) %copy-start.2) | copy-done | bytes 32792
  4.7 0.0 copy-start.3
  4.7 0.8 %copy-done.3 = f32[64,64]{1,0:T(8,128)S(1)} copy-done((f32[64,64]{1,0:T(8,128)S(1)}, f32[64,64]{1,0:T(8,128)}, u32[]{:S(2)}) %copy-start.3) | copy-done | bytes 16408
  5.4 0.0 copy-start.4
  5.4 0.7 %copy-done.4 = bf16[64,64]{1,0:T(8,128)(2,1)S(1)} copy-done((bf16[64,64]{1,0:T(8,128)(2,1)S(1)}, bf16[64,64]{1,0:T(8,128)(2,1)}, u32[]{:S(2)}) %copy-start.4) | copy-done | bytes 8216
  6.1 55.3 %shard_map.95 = (bf16[128,128]{1,0:T(8,128)(2,1)S(1)}, bf16[128,128]{1,0:T(8,128)(2,1)S(1)}) custom-call(s32[256]{0:T(256)S(1)} %copy-done.5, s32[64]{0:T(128)S(1)} %copy-done.6, s32[1]{0:T(128)S(6)} %copy.12.window_start, bf16[4,8,64,128]{3,2,1,0:T(8,128)(2,1)S(1)} %copy-done, bf16[512,128]{1,0:T(8,128)(2,1)S(1)} %bitcast.6, bf16[128,128]{1,0:T(8,128)(2,1)S(1)} %bitcast.7, ...), custom_call_target="tpu_custom_call" | custom-call | flops 1100000000 | bytes 2000000 | tf_op jit(solution)/shard_map/pallas_call | solution.py:258
  61.4 0.6 copy.13
  62.0 0.6 copy.14
Async XLA Ops:
  1.3 0.7 %copy-start.5 = (s32[256]{0:T(256)S(1)}, s32[256]{0:T(256)}, u32[]{:S(2)}) copy-start(s32[256]{0:T(256)} %time_deal.1) | copy-start | bytes 3076
  1.3 0.7 %copy-start.6 = (s32[64]{0:T(128)S(1)}, s32[64]{0:T(128)}, u32[]{:S(2)}) copy-start(s32[64]{0:T(128)} %column_times.1) | copy-start | bytes 772
  2.0 1.0 %copy-start = (bf16[4,8,64,128]{3,2,1,0:T(8,128)(2,1)S(1)}, bf16[4,8,64,128]{3,2,1,0:T(8,128)(2,1)}, u32[]{:S(2)}) copy-start(bf16[4,8,64,128]{3,2,1,0:T(8,128)(2,1)} %block_ref.1) | copy-start | bytes 1572868
  3.0 0.9 %copy-start.1 = (bf16[256,2,128]{2,1,0:T(2,128)(2,1)S(1)}, bf16[256,2,128]{2,1,0:T(2,128)(2,1)}, u32[]{:S(2)}) copy-start(bf16[256,2,128]{2,1,0:T(2,128)(2,1)} %param.9) | copy-start | bytes 393220
  3.9 0.8 %copy-start.2 = (bf16[64,2,128]{2,1,0:T(2,128)(2,1)S(1)}, bf16[64,2,128]{2,1,0:T(2,128)(2,1)}, u32[]{:S(2)}) copy-start(bf16[64,2,128]{2,1,0:T(2,128)(2,1)} %param.10) | copy-start | bytes 98308
  4.7 0.8 %copy-start.3 = (f32[64,64]{1,0:T(8,128)S(1)}, f32[64,64]{1,0:T(8,128)}, u32[]{:S(2)}) copy-start(f32[64,64]{1,0:T(8,128)} %coupling_ref.1) | copy-start | bytes 49156
  5.4 0.7 %copy-start.4 = (bf16[64,64]{1,0:T(8,128)(2,1)S(1)}, bf16[64,64]{1,0:T(8,128)(2,1)}, u32[]{:S(2)}) copy-start(bf16[64,64]{1,0:T(8,128)(2,1)} %hamiltonian_ref.1) | copy-start | bytes 24580

commit v2 on v1

v2 whole, which is shorter than its diff:
```python
import jax
import jax.numpy as jnp
from jax import lax
from jax.experimental import pallas as pl
from jax.experimental.pallas import tpu as pltpu
from jax.sharding import PartitionSpec as P


MESH = pl.DeviceIdType.MESH
BF16 = jnp.bfloat16
F32 = jnp.float32
P_SIZE = 8
TIME_STEP = 0.02
NZ = 16
NY = 4
HALF = NZ // 2
ORDER = (0, 3, 1, 2)


def halves(x):
    high = x.astype(BF16)
    return high, (x - high.astype(F32)).astype(BF16)


def dot(a, b):
    return jnp.dot(a, b, preferred_element_type=F32)


def chosen(shape, test):
    rows = lax.broadcasted_iota(jnp.int32, shape, 0)
    columns = lax.broadcasted_iota(jnp.int32, shape, 1)
    return jnp.where(test(rows, columns), 1.0, 0.0).astype(BF16)


def pair_form(small):
    spread = chosen((128, 64), lambda r, c: (r >> 1) == c)
    gather = chosen((64, 128), lambda r, c: r == (c >> 1))
    wide = dot(dot(spread, small).astype(BF16), gather)
    same = chosen((128, 128), lambda r, c: (r & 1) == (c & 1))
    return wide.astype(BF16) * same


def lane_form(small):
    spread = chosen((128, 64), lambda r, c: (r & 63) == c)
    gather = chosen((64, 128), lambda r, c: r == (c & 63))
    turned = lax.dot_general(spread, small, (((1,), (1,)), ((), ())), preferred_element_type=F32)
    return dot(turned.astype(BF16), gather).astype(BF16)


def sigma_of(x, left, right):
    count = x.shape[0] // 128
    wide = x.astype(F32)
    high, low = halves(wide * wide)
    over = dot(jnp.concatenate([high, low, high], axis=1), right)
    high, low = halves(over)
    result = []
    for n in range(count):
        rows = slice(n * 128, (n + 1) * 128)
        stacked = jnp.concatenate([high[rows], low[rows], high[rows]], axis=0)
        result.append(-(wide[rows] * dot(left, stacked)))
    return result


def kernel(
    time_hbm, column_hbm, window_hbm, block_ref, memory_hbm, panel_hbm, coupling_hbm, hamiltonian_hbm,
    rows_ref, sigma_ref,
    time_deal, column_times, window_start, memory_ref, panel_ref, coupling_ref, hamiltonian_ref,
    blocks, forms, own_sigma, old_sigma, partial, up_in, up_out, down_in, down_out, last_in, cross_out,
    load_sem, block_sem, block_send, tile_sem, first_send, pass_send,
    up_sem, down_sem, last_sem, cross_send, up_send, down_send,
):
    mem = lax.axis_index("mem")
    hist = lax.axis_index("hist")
    core = lax.rem(mem, 2)
    z = lax.rem(lax.div(mem, 2), NZ)
    x_hi = lax.div(mem, 2 * NZ)
    y = lax.div(hist, 2)
    x_lo = lax.rem(hist, 2)
    chip = mem - core
    y_next = (lax.rem(y + 1, NY), lax.rem(y + NY - 1, NY))
    y_far = lax.rem(y + 2, NY)
    z_next = (lax.rem(z + 1, NZ), lax.rem(z + NZ - 1, NZ))

    def at_mem(xx, zz):
        return xx * (2 * NZ) + zz * 2 + core

    def at_hist(yy, xx):
        return yy * 2 + xx

    def send(src, dst, send_sem, recv_sem, where):
        return pltpu.make_async_remote_copy(
            src_ref=src, dst_ref=dst, send_sem=send_sem, recv_sem=recv_sem, device_id=where, device_id_type=MESH
        )

    other_core = (chip + 1 - core, hist)
    other_x = at_hist(y, 1 - x_lo)
    peers = [other_core]
    peers += [(chip + q, other_x) for q in range(2)]
    peers += [(chip + q, at_hist(yy, x_lo)) for yy in (*y_next, y_far) for q in range(2)]
    peers += [(at_mem(xx, zz), hist) for xx in range(2) for zz in z_next]
    peers += [(at_mem(1 - x_hi, z), hist)]
    barrier = pltpu.get_barrier_semaphore()
    for peer in peers:
        pl.semaphore_signal(barrier, inc=1, device_id=peer, device_id_type=MESH)

    loads = [
        pltpu.make_async_copy(src, dst, load_sem.at[n])
        for n, (src, dst) in enumerate((
            (coupling_hbm, coupling_ref), (memory_hbm, memory_ref), (time_hbm, time_deal), (column_hbm, column_times),
            (window_hbm, window_start), (hamiltonian_hbm, hamiltonian_ref), (panel_hbm, panel_ref),
            (block_ref, blocks.at[core]),
        ))
    ]
    for copy in loads:
        copy.start()

    loads[0].wait()
    coupling_high, coupling_low = halves(coupling_ref[...])
    left_high, left_low = pair_form(coupling_high), pair_form(coupling_low)
    left = jnp.concatenate([left_high, left_high, left_low], axis=1)
    right_high, right_low = lane_form(coupling_high), lane_form(coupling_low)
    right = jnp.concatenate([right_high, right_high, right_low], axis=0)
    loads[1].wait()
    for u, tile in enumerate(sigma_of(memory_ref[...], left, right)):
        own_sigma[u % 2, u // 2] = tile.astype(BF16)

    pl.semaphore_wait(barrier, len(peers))

    mine = core * NY + y
    early = lax.div(lax.rem(2 * x_lo + 2 * NZ - z, 4), 2)
    first = []
    for n in range(2):
        u = early if n == 0 else 1 - early
        here = old_sigma.at[2 * x_lo + u, mine]
        arrival = tile_sem.at[2 * x_lo + u, mine]
        targets = []
        for yy in (y_far, *y_next):
            targets += [(q, (chip + q, at_hist(yy, x_lo))) for q in range(2)]
        targets += [(q, (chip + q, other_x)) for q in range(2)]
        targets += [(1 - core, other_core)]
        for i, (q, where) in enumerate(targets):
            copy = send(own_sigma.at[q, u], here, first_send.at[n, i], arrival, where)
            copy.start()
            first.append(copy)
        pltpu.make_async_copy(own_sigma.at[core, u], here, arrival).start()
    block_there = send(block_ref, blocks.at[core], block_send, block_sem, other_core)
    block_there.start()

    def arrived(dst, sem):
        send(dst, dst, sem, sem, other_core).wait_recv()

    sign = jnp.where(lax.broadcasted_iota(jnp.int32, (64, 128), 1) < 64, -1.0, 1.0)
    for n in (2, 3, 4):
        loads[n].wait()
    start = window_start[0]

    def build(which):
        for k in range(4):
            slot_time = time_deal[(chip + which) * 4 + k]
            for j in range(8):
                keep = (slot_time >= column_times[hist * 8 + j]) & (slot_time >= start)
                level = jnp.where(keep, 1.0, 0.0)
                tile = blocks[which, k, j].astype(F32) * level
                row = pl.multiple_of((which * 4 + k) * 128, 128)
                forms[pl.ds(row, 64), j * 128 : (j + 1) * 128] = tile.astype(BF16)
                forms[pl.ds(row + 64, 64), j * 128 : (j + 1) * 128] = (pltpu.roll(tile, 64, 1) * sign).astype(BF16)

    loads[7].wait()
    build(core)

    loads[5].wait()
    loads[6].wait()
    panel = panel_ref[...]
    applied = dot(pair_form(hamiltonian_ref[...]), panel)
    turned = pltpu.roll(applied, 64, 1) * jnp.where(lax.broadcasted_iota(jnp.int32, (128, 128), 1) < 64, 1.0, -1.0)
    base = panel.astype(F32) + TIME_STEP * turned

    def time_of(n):
        return lax.rem(z + ORDER[n], 4)

    def tile_in(t, kk):
        arrived(old_sigma.at[t, kk], tile_sem.at[t, kk])

    def pass_on(n):
        t = time_of(n)
        inside = lax.div(t, 2) == x_lo

        @pl.when(inside)
        def _():
            for q in range(2):
                kk = q * NY + y_far
                tile_in(t, kk)
                send(old_sigma.at[t, kk], old_sigma.at[t, kk], pass_send.at[t, q], tile_sem.at[t, kk], (mem, other_x)).start()

        @pl.when(jnp.logical_not(inside))
        def _():
            for q in range(2):
                kk = q * NY + y
                tile_in(t, kk)
                for d in range(2):
                    send(old_sigma.at[t, kk], old_sigma.at[t, kk], pass_send.at[t, 2 * q + d], tile_sem.at[t, kk],
                         (mem, at_hist(y_next[d], x_lo))).start()

    def complete(n):
        t = time_of(n)
        rest = jnp.where(lax.div(t, 2) == x_lo, y, y_far)
        for q in range(2):
            tile_in(t, q * NY + rest)
            for yy in y_next:
                tile_in(t, q * NY + yy)

    def multiply(n):
        t = time_of(n)
        lhs = jnp.concatenate([old_sigma[t, kk] for kk in range(8)], axis=1)
        for j in range(4):
            product = dot(lhs, forms[:, j * 256 : (j + 1) * 256])
            for i in range(2):
                partial[t, 2 * j + i] = product[:, i * 128 : (i + 1) * 128]

    def drain_passes(n):
        t = time_of(n)
        inside = lax.div(t, 2) == x_lo
        for i in range(2):
            send(old_sigma.at[t, i], old_sigma.at[t, i], pass_send.at[t, i], pass_send.at[t, i], other_core).wait_send()

        @pl.when(jnp.logical_not(inside))
        def _():
            for i in range(2, 4):
                send(old_sigma.at[t, i], old_sigma.at[t, i], pass_send.at[t, i], pass_send.at[t, i], other_core).wait_send()

    def term(zz, xx):
        return partial[lax.rem(zz, 4), 4 * xx + lax.div(zz, 4)]

    sent = {}

    def chain(d, s):
        came, went, in_sem, out_sem = ((up_in, up_out, up_sem, up_send), (down_in, down_out, down_sem, down_send))[d]
        far = lax.rem(z + HALF - s, NZ) if d == 0 else lax.rem(z + NZ - (HALF - 1) + s, NZ)
        for b in range(2):
            value = term(far, b)
            if s > 0:
                arrived(came.at[s - 1, b], in_sem.at[s - 1, b])
                value = value + came[s - 1, b].astype(F32)
            went[s, b] = value.astype(BF16)
            if s < HALF - 1 - d:
                dst, sem, where = came.at[s, b], in_sem.at[s, b], (at_mem(x_hi, z_next[d]), hist)
            else:
                dst, sem, where = last_in.at[d * 2 + x_hi], last_sem.at[d * 2 + x_hi], (at_mem(b, z_next[d]), hist)
            copy = send(went.at[s, b], dst, out_sem.at[s, b], sem, where)
            copy.start()
            sent[d, s, b] = copy

    def drain_chain(d, s):
        for b in range(2):
            sent[d, s, b].wait_send()

    pass_on(0)
    pass_on(1)
    block_there.wait_recv()
    build(1 - core)
    pass_on(2)
    complete(0)
    multiply(0)
    chain(0, 0)
    pass_on(3)
    complete(1)
    multiply(1)
    chain(0, 1)
    complete(2)
    multiply(2)
    chain(1, 0)
    complete(3)
    multiply(3)
    cross_out[...] = term(z, 1 - x_hi).astype(BF16)
    cross = send(cross_out, last_in.at[4], cross_send, last_sem.at[4], (at_mem(1 - x_hi, z), hist))
    chain(0, 2)
    chain(1, 1)
    cross.start()
    for copy in first:
        copy.wait_send()
    chain(0, 3)
    chain(1, 2)
    block_there.wait_send()
    for n in range(4):
        drain_passes(n)
    for s in range(4, HALF):
        chain(0, s)
        chain(1, s - 1)
        drain_chain(0, s - 4)
        drain_chain(1, s - 4)

    total = term(z, x_hi)
    for n in (4, 2, 3, 0, 1):
        arrived(last_in.at[n], last_sem.at[n])
        total = total + last_in[n].astype(F32)
    advanced = (base + TIME_STEP * total).astype(BF16)
    rows_ref[...] = advanced
    [new_sigma] = sigma_of(advanced, left, right)
    sigma_ref[...] = new_sigma.astype(BF16)

    cross.wait_send()
    for s in range(4, HALF):
        drain_chain(0, s)
        if s < HALF - 1:
            drain_chain(1, s)


def local(memory_block, memory_rows, panel_rows, time_deal, column_times, window_start, coupling, hamiltonian):
    tile = (128, 128)
    dma = pltpu.SemaphoreType.DMA
    vmem = pl.BlockSpec(memory_space=pltpu.VMEM)
    hbm = pl.BlockSpec(memory_space=pltpu.HBM)
    new_rows, new_sigma = pl.pallas_call(
        kernel,
        out_shape=[jax.ShapeDtypeStruct(tile, BF16)] * 2,
        in_specs=[hbm] * 8,
        out_specs=[vmem, vmem],
        scratch_shapes=[
            pltpu.SMEM(time_deal.shape, jnp.int32),
            pltpu.SMEM(column_times.shape, jnp.int32),
            pltpu.SMEM(window_start.shape, jnp.int32),
            pltpu.VMEM((512, 128), BF16),
            pltpu.VMEM(tile, BF16),
            pltpu.VMEM(coupling.shape, F32),
            pltpu.VMEM(hamiltonian.shape, BF16),
            pltpu.VMEM((2, 4, 8, 64, 128), BF16),
            pltpu.VMEM((1024, 1024), BF16),
            pltpu.VMEM((2, 2, *tile), BF16),
            pltpu.VMEM((4, 8, *tile), BF16),
            pltpu.VMEM((4, 8, *tile), F32),
            pltpu.VMEM((HALF - 1, 2, *tile), BF16),
            pltpu.VMEM((HALF, 2, *tile), BF16),
            pltpu.VMEM((HALF - 2, 2, *tile), BF16),
            pltpu.VMEM((HALF - 1, 2, *tile), BF16),
            pltpu.VMEM((5, *tile), BF16),
            pltpu.VMEM(tile, BF16),
            dma((8,)), dma, dma, dma((4, 8)), dma((2, 9)), dma((4, 4)),
            dma((HALF - 1, 2)), dma((HALF - 2, 2)), dma((5,)), dma, dma((HALF, 2)), dma((HALF - 1, 2)),
        ],
        compiler_params=pltpu.CompilerParams(
            collective_id=0, has_side_effects=True, vmem_limit_bytes=60 * 2**20
        ),
        cost_estimate=pl.CostEstimate(flops=1100000000, bytes_accessed=2000000, transcendentals=0),
    )(
        time_deal, column_times, window_start, memory_block,
        memory_rows.reshape(512, 128), panel_rows.reshape(128, 128), coupling, hamiltonian,
    )
    return new_rows.reshape(panel_rows.shape), new_sigma.reshape(panel_rows.shape)


def solution(mesh):
    in_specs = (
        P("mem", "hist", None, None),
        P(("mem", "hist"), None, None),
        P(("hist", "mem"), None, None),
        P(),
        P(),
        P(),
        P(),
        P(),
    )
    out_specs = (P(("hist", "mem"), None, None), P(("hist", "mem"), None, None))
    return jax.shard_map(local, mesh=mesh, in_specs=in_specs, out_specs=out_specs, check_vma=False)
```

time: 63.1 us -> 57.1 us (0.905)
  local copies, waits for them, and re-layouts: 6.07 us -> 2.02 us
  Pallas kernels: 55.3 us -> 52.9 us
    unnamed x16 -> x4, local copies, waits for them, and re-layouts: 6.07 us -> 2.02 us
    pallas_call x1, Pallas kernels: 55.3 us -> 52.9 us  [local(): pl.pallas_call(kernel, out_shape=[jax.ShapeDtypeStruct(tile, BF16)] * 2,...]
where the time goes in v2:
time: 57.1 us; the launch traced here: 56.2 us
  Pallas kernels  52.9 us (93%)
  local copies, waits for them, and re-layouts  2.02 us (4%)
  between operations  1.29 us (2%)
    pallas_call x1, Pallas kernels, local(): pl.pallas_call(kernel, out_shape=[jax.ShapeDtypeStruct(tile, BF16)] * 2,...  52.9 us
    unnamed x4, local copies, waits for them, and re-layouts  2.02 us

profile of v2, /device:TPU:6, one launch (start us, length us, event | category | flops | bytes accessed | tf_op | source)
XLA Modules:
  0.0 56.2 jit_solution(13253583599387653521)
XLA Ops:
  1.3 52.9 %shard_map.95 = (bf16[128,128]{1,0:T(8,128)(2,1)}, bf16[128,128]{1,0:T(8,128)(2,1)}) custom-call(s32[256]{0:T(256)} %time_hbm.1, s32[64]{0:T(128)} %column_hbm.1, s32[1]{0:T(128)S(6)} %copy.12.window_hbm, bf16[4,8,64,128]{3,2,1,0:T(8,128)(2,1)} %block_ref.1, bf16[512,128]{1,0:T(8,128)(2,1)} %bitcast.6, bf16[128,128]{1,0:T(8,128)(2,1)} %bitcast.7, ...), custom_call_target="tpu_custom_call" | custom-call | flops 1100000000 | bytes 2000000 | tf_op jit(solution)/shard_map/pallas_call | solution.py:313
  54.2 0.0 copy-start
  54.2 1.4 %copy.13 = bf16[64,2,128]{2,1,0:T(2,128)(2,1)} copy(bf16[64,2,128]{2,1,0:T(2,128)(2,1)} %bitcast.5) | data formatting | bytes 65536
  55.6 0.0 copy-done
  55.6 0.6 %copy.14 = bf16[64,2,128]{2,1,0:T(2,128)(2,1)} copy(bf16[64,2,128]{2,1,0:T(2,128)(2,1)S(1)} %bitcast.4) | data formatting | bytes 65536
Async XLA Ops:
  54.2 1.4 %copy-start = (bf16[128,128]{1,0:T(8,128)(2,1)S(1)}, bf16[128,128]{1,0:T(8,128)(2,1)}, u32[]{:S(2)}) copy-start(bf16[128,128]{1,0:T(8,128)(2,1)} %get-tuple-element.5) | copy-start | bytes 98308

commit v3 on v2

--- a/solution.py
+++ b/solution.py
@@ -13,8 +13,9 @@
 TIME_STEP = 0.02
 NZ = 16
 NY = 4
-HALF = NZ // 2
-ORDER = (0, 3, 1, 2)
+AHEAD, BEHIND = 8, 7
+PARTS = (((7, 4), (3, 1)), ((8, 5), (4, 1)))
+ORDER = (1, 0, 2, 3)
 
 
 def halves(x):
@@ -63,11 +64,11 @@
 
 def kernel(
     time_hbm, column_hbm, window_hbm, block_ref, memory_hbm, panel_hbm, coupling_hbm, hamiltonian_hbm,
-    rows_ref, sigma_ref,
+    both_ref,
     time_deal, column_times, window_start, memory_ref, panel_ref, coupling_ref, hamiltonian_ref,
-    blocks, forms, own_sigma, old_sigma, partial, up_in, up_out, down_in, down_out, last_in, cross_out,
+    blocks, forms, own_sigma, old_sigma, partial, shared_out, shared_in, chain_in, chain_out, last_in, cross_out,
     load_sem, block_sem, block_send, tile_sem, first_send, pass_send,
-    up_sem, down_sem, last_sem, cross_send, up_send, down_send,
+    shared_send, shared_sem, chain_sem, chain_send, last_sem, cross_send,
 ):
     mem = lax.axis_index("mem")
     hist = lax.axis_index("hist")
@@ -81,8 +82,8 @@
     y_far = lax.rem(y + 2, NY)
     z_next = (lax.rem(z + 1, NZ), lax.rem(z + NZ - 1, NZ))
 
-    def at_mem(xx, zz):
-        return xx * (2 * NZ) + zz * 2 + core
+    def at_mem(xx, zz, q):
+        return xx * (2 * NZ) + zz * 2 + q
 
     def at_hist(yy, xx):
         return yy * 2 + xx
@@ -97,8 +98,12 @@
     peers = [other_core]
     peers += [(chip + q, other_x) for q in range(2)]
     peers += [(chip + q, at_hist(yy, x_lo)) for yy in (*y_next, y_far) for q in range(2)]
-    peers += [(at_mem(xx, zz), hist) for xx in range(2) for zz in z_next]
-    peers += [(at_mem(1 - x_hi, z), hist)]
+    waits = len(peers) + 1 + 8
+    peers += [(at_mem(1 - x_hi, z, core), hist)]
+    for way in range(2):
+        for part in PARTS[way]:
+            source = lax.rem(z + (part[1], NZ - part[1])[way], NZ)
+            peers += [(at_mem(xx, source, way), hist) for xx in range(2)]
     barrier = pltpu.get_barrier_semaphore()
     for peer in peers:
         pl.semaphore_signal(barrier, inc=1, device_id=peer, device_id_type=MESH)
@@ -124,10 +129,10 @@
     for u, tile in enumerate(sigma_of(memory_ref[...], left, right)):
         own_sigma[u % 2, u // 2] = tile.astype(BF16)
 
-    pl.semaphore_wait(barrier, len(peers))
+    pl.semaphore_wait(barrier, waits)
 
     mine = core * NY + y
-    early = lax.div(lax.rem(2 * x_lo + 2 * NZ - z, 4), 2)
+    early = lax.div(lax.rem(2 * x_lo + 2 * NZ + 3 - z, 4), 2)
     first = []
     for n in range(2):
         u = early if n == 0 else 1 - early
@@ -215,7 +220,9 @@
         for j in range(4):
             product = dot(lhs, forms[:, j * 256 : (j + 1) * 256])
             for i in range(2):
-                partial[t, 2 * j + i] = product[:, i * 128 : (i + 1) * 128]
+                value = product[:, i * 128 : (i + 1) * 128]
+                partial[t, (2 * j + i) % 4, (2 * j + i) // 4] = value
+                shared_out[t, (2 * j + i) % 4, (2 * j + i) // 4] = value.astype(BF16)
 
     def drain_passes(n):
         t = time_of(n)
@@ -228,81 +235,125 @@
             for i in range(2, 4):
                 send(old_sigma.at[t, i], old_sigma.at[t, i], pass_send.at[t, i], pass_send.at[t, i], other_core).wait_send()
 
-    def term(zz, xx):
-        return partial[lax.rem(zz, 4), 4 * xx + lax.div(zz, 4)]
-
-    sent = {}
-
-    def chain(d, s):
-        came, went, in_sem, out_sem = ((up_in, up_out, up_sem, up_send), (down_in, down_out, down_sem, down_send))[d]
-        far = lax.rem(z + HALF - s, NZ) if d == 0 else lax.rem(z + NZ - (HALF - 1) + s, NZ)
-        for b in range(2):
-            value = term(far, b)
-            if s > 0:
-                arrived(came.at[s - 1, b], in_sem.at[s - 1, b])
-                value = value + came[s - 1, b].astype(F32)
-            went[s, b] = value.astype(BF16)
-            if s < HALF - 1 - d:
-                dst, sem, where = came.at[s, b], in_sem.at[s, b], (at_mem(x_hi, z_next[d]), hist)
-            else:
-                dst, sem, where = last_in.at[d * 2 + x_hi], last_sem.at[d * 2 + x_hi], (at_mem(b, z_next[d]), hist)
-            copy = send(went.at[s, b], dst, out_sem.at[s, b], sem, where)
-            copy.start()
-            sent[d, s, b] = copy
-
-    def drain_chain(d, s):
-        for b in range(2):
-            sent[d, s, b].wait_send()
+    def spot(way, n):
+        far = lax.rem(z + (NZ - n, n)[way], NZ)
+        return lax.rem(far, 4), lax.div(far, 4)
+
+    def term(xx):
+        t, column = spot(1, 0)
+        return partial[t, column, xx]
+
+    def share(order):
+        for way in range(2):
+
+            @pl.when(core == 1 - way)
+            def _():
+                for n in range(1, (BEHIND, AHEAD)[way] + 1):
+                    if (n if way else -n) % 4 == ORDER[order]:
+                        t, column = spot(way, n)
+                        send(shared_out.at[t, column], shared_in.at[n - 1], shared_send.at[n - 1], shared_sem.at[n - 1],
+                             other_core).start()
+
+    def drain_share(n):
+        here = shared_in.at[n - 1]
+        send(here, here, shared_send.at[n - 1], shared_send.at[n - 1], other_core).wait_send()
+
+    def chain(way, s):
+        for part, (top, end) in enumerate(PARTS[way]):
+            n = top - s
+            if n < end:
+                continue
+            t, column = spot(way, n)
+            beyond = lax.rem(z + (NZ - end, end)[way], NZ)
+            for i in range(2):
+                q = (core, 1 - core)[i]
+                if i == 1:
+                    arrived(shared_in.at[n - 1], shared_sem.at[n - 1])
+                for b in range(2):
+                    value = partial[t, column, b] if i == 0 else shared_in[n - 1, b].astype(F32)
+                    if s > 0:
+                        arrived(chain_in.at[n - 1, i, b], chain_sem.at[n - 1, i, b])
+                        value = value + chain_in[n - 1, i, b].astype(F32)
+                    chain_out[n - 1, i, b] = value.astype(BF16)
+                    if n > end:
+                        dst, sem = chain_in.at[n - 2, i, b], chain_sem.at[n - 2, i, b]
+                        where = (at_mem(x_hi, z_next[1 - way], core), hist)
+                    else:
+                        slot = 4 * way + 2 * part + x_hi
+                        dst, sem, where = last_in.at[slot], last_sem.at[slot], (at_mem(b, beyond, q), hist)
+                    send(chain_out.at[n - 1, i, b], dst, chain_send.at[n - 1, i, b], sem, where).start()
+
+    def drain_chain(n):
+        for i in range(2):
+            for b in range(2):
+                here = chain_out.at[n - 1, i, b]
+                send(here, here, chain_send.at[n - 1, i, b], chain_send.at[n - 1, i, b], other_core).wait_send()
+
+    def step(n):
+        complete(n)
+        multiply(n)
+        share(n)
 
     pass_on(0)
     pass_on(1)
     block_there.wait_recv()
     build(1 - core)
     pass_on(2)
-    complete(0)
-    multiply(0)
-    chain(0, 0)
     pass_on(3)
-    complete(1)
-    multiply(1)
-    chain(0, 1)
-    complete(2)
-    multiply(2)
-    chain(1, 0)
-    complete(3)
-    multiply(3)
-    cross_out[...] = term(z, 1 - x_hi).astype(BF16)
-    cross = send(cross_out, last_in.at[4], cross_send, last_sem.at[4], (at_mem(1 - x_hi, z), hist))
-    chain(0, 2)
-    chain(1, 1)
+    step(0)
+    pl.when(core == 0)(lambda: chain(0, 0))
+    step(1)
+    cross_out[...] = term(1 - x_hi).astype(BF16)
+    cross = send(cross_out, last_in.at[8], cross_send, last_sem.at[8], (at_mem(1 - x_hi, z, core), hist))
     cross.start()
-    for copy in first:
+    pl.when(core == 1)(lambda: chain(1, 0))
+    step(2)
+    pl.when(core == 0)(lambda: chain(0, 1))
+    step(3)
+
+    @pl.when(core == 1)
+    def _():
+        for s in range(1, 4):
+            chain(1, s)
+        for n in range(1, BEHIND + 1):
+            drain_share(n)
+        for n in (8, 7, 4, 3):
+            drain_chain(n)
+
+    @pl.when(core == 0)
+    def _():
+        for s in range(2, 4):
+            chain(0, s)
+        for n in range(1, AHEAD + 1):
+            drain_share(n)
+        for n in (7, 6, 3, 2):
+            drain_chain(n)
+
+    for copy in first + [block_there]:
         copy.wait_send()
-    chain(0, 3)
-    chain(1, 2)
-    block_there.wait_send()
     for n in range(4):
         drain_passes(n)
-    for s in range(4, HALF):
-        chain(0, s)
-        chain(1, s - 1)
-        drain_chain(0, s - 4)
-        drain_chain(1, s - 4)
-
-    total = term(z, x_hi)
-    for n in (4, 2, 3, 0, 1):
+
+    total = term(x_hi)
+    for n in (8, 2, 3, 6, 7, 0, 1, 4, 5):
         arrived(last_in.at[n], last_sem.at[n])
         total = total + last_in[n].astype(F32)
     advanced = (base + TIME_STEP * total).astype(BF16)
-    rows_ref[...] = advanced
+    both_ref[0] = advanced
     [new_sigma] = sigma_of(advanced, left, right)
-    sigma_ref[...] = new_sigma.astype(BF16)
+    both_ref[1] = new_sigma.astype(BF16)
 
     cross.wait_send()
-    for s in range(4, HALF):
-        drain_chain(0, s)
-        if s < HALF - 1:
-            drain_chain(1, s)
+
+    @pl.when(core == 0)
+    def _():
+        for n in (5, 4, 1):
+            drain_chain(n)
+
+    @pl.when(core == 1)
+    def _():
+        for n in (6, 5, 2, 1):
+            drain_chain(n)
 
 
 def local(memory_block, memory_rows, panel_rows, time_deal, column_times, window_start, coupling, hamiltonian):
@@ -310,11 +361,11 @@
     dma = pltpu.SemaphoreType.DMA
     vmem = pl.BlockSpec(memory_space=pltpu.VMEM)
     hbm = pl.BlockSpec(memory_space=pltpu.HBM)
-    new_rows, new_sigma = pl.pallas_call(
+    both = pl.pallas_call(
         kernel,
-        out_shape=[jax.ShapeDtypeStruct(tile, BF16)] * 2,
+        out_shape=jax.ShapeDtypeStruct((2, *tile), BF16),
         in_specs=[hbm] * 8,
-        out_specs=[vmem, vmem],
+        out_specs=vmem,
         scratch_shapes=[
             pltpu.SMEM(time_deal.shape, jnp.int32),
             pltpu.SMEM(column_times.shape, jnp.int32),
@@ -327,15 +378,15 @@
             pltpu.VMEM((1024, 1024), BF16),
             pltpu.VMEM((2, 2, *tile), BF16),
             pltpu.VMEM((4, 8, *tile), BF16),
-            pltpu.VMEM((4, 8, *tile), F32),
-            pltpu.VMEM((HALF - 1, 2, *tile), BF16),
-            pltpu.VMEM((HALF, 2, *tile), BF16),
-            pltpu.VMEM((HALF - 2, 2, *tile), BF16),
-            pltpu.VMEM((HALF - 1, 2, *tile), BF16),
-            pltpu.VMEM((5, *tile), BF16),
+            pltpu.VMEM((4, 4, 2, *tile), F32),
+            pltpu.VMEM((4, 4, 2, *tile), BF16),
+            pltpu.VMEM((AHEAD, 2, *tile), BF16),
+            pltpu.VMEM((AHEAD - 1, 2, 2, *tile), BF16),
+            pltpu.VMEM((AHEAD, 2, 2, *tile), BF16),
+            pltpu.VMEM((9, *tile), BF16),
             pltpu.VMEM(tile, BF16),
             dma((8,)), dma, dma, dma((4, 8)), dma((2, 9)), dma((4, 4)),
-            dma((HALF - 1, 2)), dma((HALF - 2, 2)), dma((5,)), dma, dma((HALF, 2)), dma((HALF - 1, 2)),
+            dma((AHEAD,)), dma((AHEAD,)), dma((AHEAD - 1, 2, 2)), dma((AHEAD, 2, 2)), dma((9,)), dma,
         ],
         compiler_params=pltpu.CompilerParams(
             collective_id=0, has_side_effects=True, vmem_limit_bytes=60 * 2**20
@@ -345,7 +396,7 @@
         time_deal, column_times, window_start, memory_block,
         memory_rows.reshape(512, 128), panel_rows.reshape(128, 128), coupling, hamiltonian,
     )
-    return new_rows.reshape(panel_rows.shape), new_sigma.reshape(panel_rows.shape)
+    return both[0].reshape(panel_rows.shape), both[1].reshape(panel_rows.shape)
 
 
 def solution(mesh):

time: 57.1 us -> 52.8 us (0.925); the launches traced: 56.2 us -> 52.6 us
  Pallas kernels: 52.9 us -> 49.9 us
  local copies, waits for them, and re-layouts: 2.02 us -> 1.4 us
    pallas_call x1, Pallas kernels: 52.9 us -> 49.9 us  [local(): pl.pallas_call(kernel, out_shape=jax.ShapeDtypeStruct((2, *tile), BF16),...]
    unnamed x4 -> x0, local copies, waits for them, and re-layouts: 2.02 us -> none
    slice x0 -> x1, local copies, waits for them, and re-layouts: none -> 1.4 us  [local(): both[1].reshape(panel_rows.shape)]
where the time goes in v3:
time: 52.8 us; the launch traced here: 52.6 us
  Pallas kernels  49.9 us (95%)
  local copies, waits for them, and re-layouts  1.4 us (3%)
  between operations  1.29 us (2%)
    pallas_call x1, Pallas kernels, local(): pl.pallas_call(kernel, out_shape=jax.ShapeDtypeStruct((2, *tile), BF16),...  49.9 us
    slice x1, local copies, waits for them, and re-layouts, local(): both[1].reshape(panel_rows.shape)  1.4 us

profile of v3, /device:TPU:6, one launch (start us, length us, event | category | flops | bytes accessed | tf_op | source)
XLA Modules:
  0.0 52.6 jit_solution(9606507614644098218)
XLA Ops:
  1.3 49.9 %shard_map.95 = bf16[2,128,128]{2,1,0:T(8,128)(2,1)} custom-call(s32[256]{0:T(256)} %time_hbm.1, s32[64]{0:T(128)} %column_hbm.1, s32[1]{0:T(128)S(6)} %copy.10.window_hbm, bf16[4,8,64,128]{3,2,1,0:T(8,128)(2,1)} %block_ref.1, bf16[512,128]{1,0:T(8,128)(2,1)} %bitcast.6, bf16[128,128]{1,0:T(8,128)(2,1)} %bitcast.7, f32[64,64]{1,0:T(8,128)} %coupling_hbm.1, ...), custom_call_target="tpu_custom_call" | custom-call | flops 1100000000 | bytes 2000000 | tf_op jit(solution)/shard_map/pallas_call | solution.py:364
  51.2 1.4 %fusion = (bf16[1,128,128]{2,1,0:T(8,128)(2,1)}, bf16[1,128,128]{2,1,0:T(8,128)(2,1)}) fusion(bf16[2,128,128]{2,1,0:T(8,128)(2,1)} %shard_map.95), kind=kLoop, calls=%fused_computation | loop fusion | bytes 131072 | tf_op jit(solution)/shard_map/slice | solution.py:399

commit v4 on v3

--- a/solution.py
+++ b/solution.py
@@ -301,15 +301,15 @@
     pass_on(2)
     pass_on(3)
     step(0)
-    pl.when(core == 0)(lambda: chain(0, 0))
     step(1)
     cross_out[...] = term(1 - x_hi).astype(BF16)
     cross = send(cross_out, last_in.at[8], cross_send, last_sem.at[8], (at_mem(1 - x_hi, z, core), hist))
     cross.start()
+    pl.when(core == 0)(lambda: chain(0, 0))
+    step(2)
     pl.when(core == 1)(lambda: chain(1, 0))
-    step(2)
+    step(3)
     pl.when(core == 0)(lambda: chain(0, 1))
-    step(3)
 
     @pl.when(core == 1)
     def _():

time: 52.8 us -> 50.4 us (0.955)
  Pallas kernels: 49.9 us -> 47.5 us
    pallas_call x1, Pallas kernels: 49.9 us -> 47.5 us  [local(): pl.pallas_call(kernel, out_shape=jax.ShapeDtypeStruct((2, *tile), BF16),...]
where the time goes in v4:
time: 50.4 us; the launch traced here: 50.2 us
  Pallas kernels  47.5 us (94%)
  local copies, waits for them, and re-layouts  1.4 us (3%)
  between operations  1.29 us (3%)
    pallas_call x1, Pallas kernels, local(): pl.pallas_call(kernel, out_shape=jax.ShapeDtypeStruct((2, *tile), BF16),...  47.5 us
    slice x1, local copies, waits for them, and re-layouts, local(): both[1].reshape(panel_rows.shape)  1.4 us

profile of v4, /device:TPU:6, one launch (start us, length us, event | category | flops | bytes accessed | tf_op | source)
XLA Modules:
  0.0 50.2 jit_solution(15454415497074327489)
XLA Ops:
  1.3 47.5 %shard_map.95 = bf16[2,128,128]{2,1,0:T(8,128)(2,1)} custom-call(s32[256]{0:T(256)} %time_hbm.1, s32[64]{0:T(128)} %column_hbm.1, s32[1]{0:T(128)S(6)} %copy.10.window_hbm, bf16[4,8,64,128]{3,2,1,0:T(8,128)(2,1)} %block_ref.1, bf16[512,128]{1,0:T(8,128)(2,1)} %bitcast.6, bf16[128,128]{1,0:T(8,128)(2,1)} %bitcast.7, f32[64,64]{1,0:T(8,128)} %coupling_hbm.1, ...), custom_call_target="tpu_custom_call" | custom-call | flops 1100000000 | bytes 2000000 | tf_op jit(solution)/shard_map/pallas_call | solution.py:364
  48.8 1.4 %fusion = (bf16[1,128,128]{2,1,0:T(8,128)(2,1)}, bf16[1,128,128]{2,1,0:T(8,128)(2,1)}) fusion(bf16[2,128,128]{2,1,0:T(8,128)(2,1)} %shard_map.95), kind=kLoop, calls=%fused_computation | loop fusion | bytes 131072 | tf_op jit(solution)/shard_map/slice | solution.py:399
